TPU v7x, 128 devices: a whole 4x4x4 slice. The times are simulated.
128 devices in a mesh: rows: 32 (over x, z, core), cols: 4 (over y).
Axes of the slice: x: 4, y: 4, z: 4, core: 2. Of those that a mesh axis runs over, the one named last changes fastest.
Arguments:
- panel: float32 [524288, 256], P(('rows', 'cols')), as said below
- trailing: float32 [524288, 512], P('rows', 'cols'), may hold values from -6 to 6
Outputs:
- r_factor: float32 [256, 256], replicated
- r_cross: float32 [256, 512], P(None, 'cols')
- residual: float32 [524288, 512], P('rows', 'cols')
Inputs may be any that keep to these rules, and one draw needn't show every extreme that they name: The panel has full rank and is well conditioned.
All inputs are finite; a program needn't handle non-finite values.
Results may differ from a plain program's by a relative error of at most 0.0003.
Values sent between devices are 32-bit elements; how exact they have to be, the bound alone decides.
A program may use at most 256 MiB of HBM per device.

v0:
```python
import jax
import jax.numpy as jnp
from jax import lax
from jax.sharding import PartitionSpec as P


def product(left, right):
    return jnp.dot(left, right, precision=lax.Precision.HIGHEST, preferred_element_type=jnp.float32)


def project(lower, cross):
    r_block = lax.linalg.triangular_solve(lower, cross, left_side=True, lower=True)
    coeff = lax.linalg.triangular_solve(
        lower, r_block, left_side=True, lower=True, transpose_a=True
    )
    return (r_block, coeff)


def per_device(panel, trailing):
    local_gram = product(panel.T, panel)
    gram = lax.psum(local_gram, ("rows", "cols"))
    lower = jnp.linalg.cholesky(gram)
    r_factor = lower.T
    full_panel = lax.all_gather(panel, "cols", axis=0, tiled=True)
    cross = lax.psum(product(full_panel.T, trailing), "rows")
    r_cross, coeff = project(lower, cross)
    residual = trailing - product(full_panel, coeff)
    return (r_factor, r_cross, residual)


def solution(mesh):
    return jax.shard_map(
        per_device,
        mesh=mesh,
        in_specs=(P(("rows", "cols"), None), P("rows", "cols")),
        out_specs=(P(), P(None, "cols"), P("rows", "cols")),
        check_vma=False,
    )
```

profile of v0, /device:TPU:1, one launch (start us, length us, event | category | flops | bytes accessed | tf_op | source)
XLA Modules:
  0.0 500.4 jit_solution(9829354825001235231)
XLA Ops:
  8.0 10.9 %fusion.19 = f32[256,256]{0,1:T(8,128)} fusion(f32[4096,256]{1,0:T(8,128)} %param.2), kind=kOutput, calls=%fused_computation.41 | convolution fusion | flops 3221225472 | bytes 4456448 | tf_op jit(solution)/shard_map/dot_general | solution.py:8
  19.0 0.5 all-gather.2.cloned.1.call-update
  19.5 0.2 all-reduce.6.cloned.1.call-start
  19.8 9.0 %copy.7 = f32[16384,128]{0,1:T(8,128)} copy(f32[16384,128]{1,0:T(8,128)} %param.3) | data formatting | bytes 16777216 | tf_op args[1]
  28.8 260.3 %all-reduce.4.cloned.1.call-done = f32[256,256]{0,1:T(8,128)} async-done(((f32[256,256]{0,1:T(8,128)}), f32[256,256]{0,1:T(8,128)}) %all-reduce.4.cloned.1.call-update) | async-done | bytes 262160 | tf_op jit(solution)/shard_map/psum | solution.py:21
  289.1 1.1 copy.6
  290.2 1.0 fusion.1
  291.2 11.7 %cholesky.50 = f32[128,128]{1,0:T(8,128)S(1)} custom-call(f32[128,128]{1,0:T(8,128)S(1)} %cholesky.118), custom_call_target="Cholesky" | custom-call | tf_op jit(solution)/shard_map/jit(cholesky)/cholesky | solution.py:22
  302.9 9.8 %custom-call.16 = f32[1,128,128]{1,2,0:T(8,128)S(1)} custom-call(f32[1,128,128]{2,1,0:T(8,128)S(1)} %get-tuple-element.29), custom_call_target="InvertDiagBlocksLowerTriangular" | custom-call | tf_op jit(solution)/shard_map/jit(cholesky)/cholesky | solution.py:22
  312.8 0.2 constant_dynamic-update-slice_fusion.1
  313.0 0.3 convolution_subtract_fusion.2
  313.2 11.7 %cholesky.105 = f32[128,128]{1,0:T(8,128)S(1)} custom-call(f32[128,128]{1,0:T(8,128)S(1)} %convolution_subtract_fusion.2), custom_call_target="Cholesky" | custom-call | tf_op jit(solution)/shard_map/jit(cholesky)/cholesky | solution.py:22
  325.0 0.6 compare_reduce_fusion
  327.0 31.1 %fusion.20 = f32[256,128]{1,0:T(8,128)} fusion(f32[16384,256]{1,0:T(8,128)} %all-gather.2.cloned.1.call-done, f32[16384,128]{1,0:T(8,128)} %param.3), kind=kOutput, calls=%fused_computation.42 | convolution fusion | flops 6442450944 | bytes 25296896 | tf_op jit(solution)/shard_map/dot_general | solution.py:8
  358.2 0.1 triangular_solve.53
  358.2 4.1 while.1
  358.3 0.6 fusion.34
  358.8 1.4 bitcast_dynamic-update-slice_fusion.2
  360.3 0.6 fusion.34
  360.9 1.4 bitcast_dynamic-update-slice_fusion.2
  362.3 0.8 copy.8
  363.2 19.9 %custom-call.17 = f32[2,128,128]{1,2,0:T(8,128)S(1)} custom-call(f32[2,128,128]{2,1,0:T(8,128)S(1)} %get-tuple-element.10), custom_call_target="InvertDiagBlocksLowerTriangular" | custom-call | tf_op jit(solution)/shard_map/triangular_solve | solution.py:12
  383.1 72.3 %all-reduce.6.cloned.1.call-done = f32[256,128]{1,0:T(8,128)} async-done(((f32[256,128]{1,0:T(8,128)}), f32[256,128]{1,0:T(8,128)}) %all-reduce.6.cloned.1.call-update) | async-done | bytes 131088 | tf_op jit(solution)/shard_map/psum | solution.py:25
  455.4 1.1 fusion.7
  456.5 1.0 convolution_subtract_fusion.1
  457.6 0.3 fusion.14
  457.9 0.2 fusion.13
  458.1 0.7 pad_maximum_fusion
  458.8 0.3 convolution_subtract_fusion
  459.1 0.2 fusion.12
  459.3 24.3 %fusion = f32[16384,128]{0,1:T(8,128)} fusion(f32[16384,128]{0,1:T(8,128)} %copy.7, f32[16384,256]{1,0:T(8,128)} %all-gather.2.cloned.1.call-done, f32[128,128]{1,0:T(8,128)S(1)} %fusion.13, f32[128,128]{1,0:T(8,128)S(1)} %fusion.12), kind=kOutput, calls=%fused_computation.3 | convolution fusion | flops 6444580864 | bytes 33685504 | tf_op jit(solution)/shard_map/dot_general | solution.py:8
  483.5 9.0 %copy.9 = f32[16384,128]{1,0:T(8,128)} copy(f32[16384,128]{0,1:T(8,128)} %fusion) | data formatting | bytes 16777216
  (14 shorter events, 0.3 us)
Async XLA Ops:
  8.0 281.1 %all-reduce.4.cloned.1.call-start = ((), (), s32[]{:S(2)}) async-start(), calls=%async_computation | async-start | bytes 524288 | tf_op jit(solution)/shard_map/psum | solution.py:21
  19.0 308.1 %all-gather.2.cloned.1.call-start = ((), (), s32[]{:S(2)}) async-start(), calls=%async_computation.1 | async-start | bytes 20971520 | tf_op jit(solution)/shard_map/all_gather | solution.py:24
  19.5 435.9 %all-reduce.6.cloned.1.call-start = ((), (), s32[]{:S(2)}) async-start(), calls=%async_computation.2 | async-start | bytes 262144 | tf_op jit(solution)/shard_map/psum | solution.py:25
Sparse Core Ops, SparseCore 0:
  19.1 269.9 all-reduce.3
Sparse Core Ops, SparseCore 1:
  21.1 157.0 all-gather.1
  358.3 97.1 all-reduce.5
where the time goes:
time: 506 us; the launch traced here: 500 us
  waiting for transfers between devices  333 us (66%)
  matrix products  69.9 us (14%)
  other arithmetic  55.6 us (11%)
  local copies, waits for them, and re-layouts  24 us (5%)
  between operations  17.4 us (3%)
    psum x1, waiting for transfers between devices, per_device(): gram = lax.psum(local_gram, ('rows', 'cols'))  260 us
    psum x1, waiting for transfers between devices, per_device(): cross = lax.psum(product(full_panel.T, trailing), 'rows')  72.3 us
    dot_general x3, matrix products, product(): jnp.dot(left, right, precision=lax.Precision.HIGHEST, preferred_element_t...  66.3 us
    another operation x6, other arithmetic, per_device(): lower = jnp.linalg.cholesky(gram)  34 us
    another operation x4, other arithmetic, project(): lax.linalg.triangular_solve(lower, cross, left_side=True, lower=True)  20.6 us
    unnamed x3, local copies, waits for them, and re-layouts  18.8 us
  transfers between devices with their start and end apart: 3, of which 2 were waited for; matrix products, arithmetic and copies ran while one was open for 14% of the time, Pallas kernels for 0%

commit v1 on v0

v1 whole, which is shorter than its diff:
```python
import functools

import jax
import jax.numpy as jnp
from jax import lax
from jax.experimental import pallas as pl
from jax.experimental.pallas import tpu as pltpu
from jax.sharding import PartitionSpec as P

MESH = pl.DeviceIdType.MESH
BLOCK = 32


def split(x):
    high = x.astype(jnp.bfloat16)
    return high, (x - high.astype(jnp.float32)).astype(jnp.bfloat16)


def dot(a, b):
    return jnp.dot(a, b, preferred_element_type=jnp.float32)


def exact(a, b, dims):
    return lax.dot_general(
        a, b, (dims, ((), ())), precision=lax.Precision.HIGHEST, preferred_element_type=jnp.float32
    )


def loop(n, body):
    def step(i, carry):
        body(i)
        return carry

    lax.fori_loop(0, n, step, 0)


def factor(work, width):
    def block_step(k, carry):
        first = pl.multiple_of(k * BLOCK, BLOCK)
        rows = work[pl.ds(first, BLOCK), :]
        row_at = lax.broadcasted_iota(jnp.int32, (BLOCK, 1), 0)
        lane_at = lax.broadcasted_iota(jnp.int32, (BLOCK, width), 1)
        for j in range(BLOCK):
            column = jnp.sum(
                jnp.where(lane_at == first + j, rows[:, :width], 0.0), axis=1, keepdims=True
            )
            pivot = column[j : j + 1, :]
            scale = lax.rsqrt(pivot)
            scale = scale * (1.5 - 0.5 * pivot * scale * scale)
            pivot_row = rows[j : j + 1, :] * scale
            below = jnp.where(row_at > j, column * scale, 0.0)
            rows = jnp.where(row_at == j, pivot_row, rows - below * pivot_row)
        work[pl.ds(first, BLOCK), :] = rows
        later = jnp.where(lane_at >= first + BLOCK, rows[:, :width], 0.0)
        work[...] -= exact(later, rows, ((0,), (0,)))
        return carry

    lax.fori_loop(0, width // BLOCK, block_step, 0)


def kernel(
    groups, chunk,
    panel, trailing, r_factor, r_cross, residual,
    held, trail, high, low, turned, gram, gram_in, gram_y, gram_all, work, both,
    acc, cross_out, cross_in, cross_all,
    own_sem, trail_sem, out_sem,
    send_r, send_l, recv_l, recv_r, pass_send_r, pass_send_l, pass_recv_l, pass_recv_r,
    small_send, small_recv,
):
    width = panel.shape[1]
    columns = trailing.shape[1]
    own = panel.shape[0] // chunk
    half = own // 2
    chunks = trailing.shape[0] // chunk
    part = width // groups
    me = lax.axis_index("rows")
    y = lax.axis_index("cols")
    sides = trailing.shape[0] // panel.shape[0]
    right = lax.rem(y + 1, sides)
    left = lax.rem(y + sides - 1, sides)
    across = lax.rem(y + 2, sides)

    def load_panel(c):
        return pltpu.make_async_copy(
            panel.at[pl.ds(c * chunk, chunk)], held.at[y * own + c], own_sem.at[c]
        )

    def load_trail(c):
        return pltpu.make_async_copy(
            trailing.at[pl.ds(c * chunk, chunk)], trail.at[c], trail_sem.at[c]
        )

    def store(c):
        return pltpu.make_async_copy(
            trail.at[c], residual.at[pl.ds(c * chunk, chunk)], out_sem.at[c]
        )

    loop(own, lambda c: load_panel(c).start())
    loop(chunks, lambda c: load_trail(c).start())

    def peer(d):
        return lax.rem(me + d + 1, groups)

    def side(d):
        return lax.rem(y + d + 1, sides)

    barrier = pltpu.get_barrier_semaphore()
    loop(sides - 1, lambda d: pl.semaphore_signal(
        barrier, inc=1, device_id={"cols": side(d)}, device_id_type=MESH))
    loop(groups - 1, lambda d: pl.semaphore_signal(
        barrier, inc=1, device_id={"rows": peer(d)}, device_id_type=MESH))
    pl.semaphore_wait(barrier, groups + sides - 2)

    def copy_y(src, dst, send, recv, to):
        return pltpu.make_async_remote_copy(
            src_ref=src, dst_ref=dst, send_sem=send, recv_sem=recv,
            device_id={"cols": to}, device_id_type=MESH)

    def to_right(c):
        return copy_y(panel.at[pl.ds(c * chunk, chunk)], held.at[y * own + c],
                      send_r.at[c], recv_l.at[c], right)

    def to_left(c):
        return copy_y(panel.at[pl.ds(c * chunk, chunk)], held.at[y * own + c],
                      send_l.at[c], recv_r.at[c], left)

    def from_left(c):
        return copy_y(held.at[left * own + c], held.at[left * own + c],
                      send_r.at[c], recv_l.at[c], right)

    def from_right(c):
        return copy_y(held.at[right * own + c], held.at[right * own + c],
                      send_l.at[c], recv_r.at[c], left)

    def pass_right(c):
        return copy_y(held.at[left * own + c], held.at[left * own + c],
                      pass_send_r.at[c], pass_recv_l.at[c], right)

    def pass_left(c):
        return copy_y(held.at[right * own + half + c], held.at[right * own + half + c],
                      pass_send_l.at[c], pass_recv_r.at[c], left)

    def passed_left(c):
        return copy_y(held.at[across * own + c], held.at[across * own + c],
                      pass_send_r.at[c], pass_recv_l.at[c], right)

    def passed_right(c):
        return copy_y(held.at[across * own + half + c], held.at[across * own + half + c],
                      pass_send_l.at[c], pass_recv_r.at[c], left)

    def send_own(c):
        to_right(c).start()
        to_left(lax.rem(c + half, own)).start()

    loop(own, send_own)

    gram[...] = jnp.zeros_like(gram)
    both[...] = jnp.zeros_like(both)

    def gram_step(c):
        load_panel(c).wait()
        at = y * own + c
        x = held[at]
        x_high, x_low = split(x)
        high[at] = x_high
        low[at] = x_low
        x_turned = x.T.astype(jnp.bfloat16)
        gram[...] += dot(x_turned, x_high)
        both[:width, :] += dot(x_turned, x_low)

    loop(own, gram_step)
    mixed = both[:width, :]
    gram[...] += mixed + mixed.T

    def spread(src_of, dst, stage):
        def one(d):
            to = peer(d)
            pltpu.make_async_remote_copy(
                src_ref=src_of(to), dst_ref=dst.at[me],
                send_sem=small_send.at[stage], recv_sem=small_recv.at[stage],
                device_id={"rows": to}, device_id_type=MESH).start()

        loop(groups - 1, one)

    def spread_wait(dst, stage):
        some = dst.at[pl.ds(0, groups - 1)]
        everything = pltpu.make_async_remote_copy(
            src_ref=some, dst_ref=some,
            send_sem=small_send.at[stage], recv_sem=small_recv.at[stage],
            device_id={"rows": peer(0)}, device_id_type=MESH)
        everything.wait()

    spread(lambda to: gram.at[pl.ds(pl.multiple_of(to * part, 8), part)], gram_in, 0)
    gram_in[me] = gram[pl.ds(pl.multiple_of(me * part, 8), part), :]

    def turn(c):
        load_trail(c).wait()
        t_high, t_low = split(trail[c].T)
        turned[c, :columns, :] = t_high
        turned[c, columns:, :] = t_low

    loop(chunks, turn)
    spread_wait(gram_in, 0)
    gram_y[y] = jnp.sum(gram_in[...], axis=0)

    def over_y(d):
        return copy_y(gram_y.at[y], gram_y.at[y], small_send.at[1], small_recv.at[1], side(d))

    loop(sides - 1, lambda d: over_y(d).start())

    acc[...] = jnp.zeros_like(acc)

    def add_cross(at):
        product = dot(turned[at], high[at])
        acc[...] += product[:columns] + (
            product[columns:] + dot(turned[at, :columns, :], low[at]))

    loop(own, lambda c: add_cross(y * own + c))

    some = gram_y.at[pl.ds(0, sides - 1)]
    copy_y(some, some, small_send.at[1], small_recv.at[1], right).wait()
    gram_all[me] = jnp.sum(gram_y[...], axis=0)
    spread(lambda to: gram_all.at[me], gram_all, 2)
    spread_wait(gram_all, 2)

    row_at = lax.broadcasted_iota(jnp.int32, (width, width), 0)
    col_at = lax.broadcasted_iota(jnp.int32, (width, width), 1)
    work[:, :width] = gram_all[...].reshape(width, width)
    work[:, width:] = jnp.where(row_at == col_at, 1.0, 0.0)
    factor(work, width)
    r_factor[...] = jnp.where(row_at <= col_at, work[:, :width], 0.0)
    inverse = work[:, width:]
    both[:width, :] = inverse
    both[width:, :] = exact(inverse, inverse, ((0,), (0,)))

    def take(at):
        x_high, x_low = split(held[at])
        high[at] = x_high
        low[at] = x_low
        add_cross(at)

    def first_half(c):
        from_left(c).wait_recv()
        pass_right(c).start()
        from_right(half + c).wait_recv()
        pass_left(c).start()
        take(left * own + c)
        take(right * own + half + c)

    def second_half(c):
        from_left(half + c).wait_recv()
        take(left * own + half + c)
        from_right(c).wait_recv()
        take(right * own + c)

    def passed(c):
        passed_left(c).wait_recv()
        take(across * own + c)
        passed_right(c).wait_recv()
        take(across * own + half + c)

    loop(half, first_half)
    loop(half, second_half)
    loop(half, passed)

    for side_at in range(width // 128):
        cross_out[pl.ds(side_at * columns, columns), :] = acc[:, side_at * 128 : side_at * 128 + 128]
    spread(lambda to: cross_out.at[pl.ds(pl.multiple_of(to * part, 8), part)], cross_in, 3)
    cross_in[me] = cross_out[pl.ds(pl.multiple_of(me * part, 8), part), :]
    spread_wait(cross_in, 3)
    cross_all[me] = jnp.sum(cross_in[...], axis=0)
    spread(lambda to: cross_all.at[me], cross_all, 4)
    spread_wait(cross_all, 4)

    flat = cross_all[...].reshape(width, columns)
    cross = jnp.concatenate([flat[:columns], flat[columns:]], axis=1)
    solved = exact(both[...], cross, ((1,), (1,)))
    r_cross[...] = solved[:width]
    c_high, c_low = split(solved[width:])
    c_both = jnp.concatenate([c_high, c_low], axis=1)

    def project(c):
        product = dot(high[c], c_both)
        rest = product[:, columns:] + dot(low[c], c_high)
        trail[c] = trail[c] - (product[:, :columns] + rest)
        store(c).start()

    loop(chunks, project)

    def finish(c):
        to_right(c).wait_send()
        to_left(c).wait_send()

    loop(own, finish)

    def finish_passed(c):
        pass_right(c).wait_send()
        pass_left(c).wait_send()

    loop(half, finish_passed)
    loop(chunks, lambda c: store(c).wait())


def per_device(groups, chunk, panel, trailing):
    rows, width = panel.shape
    total, columns = trailing.shape
    own, chunks, part = rows // chunk, total // chunk, width // groups
    half = own // 2
    sides = total // rows
    f32, bf16 = jnp.float32, jnp.bfloat16
    dma = pltpu.SemaphoreType.DMA
    return pl.pallas_call(
        functools.partial(kernel, groups, chunk),
        out_shape=(
            jax.ShapeDtypeStruct((width, width), f32),
            jax.ShapeDtypeStruct((width, columns), f32),
            jax.ShapeDtypeStruct((total, columns), f32),
        ),
        in_specs=[pl.BlockSpec(memory_space=pl.ANY)] * 2,
        out_specs=(
            pl.BlockSpec(memory_space=pltpu.VMEM),
            pl.BlockSpec(memory_space=pltpu.VMEM),
            pl.BlockSpec(memory_space=pl.ANY),
        ),
        scratch_shapes=[
            pltpu.VMEM((chunks, chunk, width), f32),
            pltpu.VMEM((chunks, chunk, columns), f32),
            pltpu.VMEM((chunks, chunk, width), bf16),
            pltpu.VMEM((chunks, chunk, width), bf16),
            pltpu.VMEM((chunks, 2 * columns, chunk), bf16),
            pltpu.VMEM((width, width), f32),
            pltpu.VMEM((groups, part, width), f32),
            pltpu.VMEM((sides, part, width), f32),
            pltpu.VMEM((groups, part, width), f32),
            pltpu.VMEM((width, 2 * width), f32),
            pltpu.VMEM((2 * width, width), f32),
            pltpu.VMEM((columns, width), f32),
            pltpu.VMEM((width, columns), f32),
            pltpu.VMEM((groups, part, columns), f32),
            pltpu.VMEM((groups, part, columns), f32),
            dma((own,)), dma((chunks,)), dma((chunks,)),
            dma((own,)), dma((own,)), dma((own,)), dma((own,)),
            dma((half,)), dma((half,)), dma((half,)), dma((half,)),
            dma((5,)), dma((5,)),
        ],
        compiler_params=pltpu.CompilerParams(
            collective_id=0, has_side_effects=True, vmem_limit_bytes=60 * 2**20
        ),
    )(panel, trailing)


def solution(mesh):
    return jax.shard_map(
        functools.partial(per_device, mesh.shape["rows"], 512),
        mesh=mesh,
        in_specs=(P(("rows", "cols"), None), P("rows", "cols")),
        out_specs=(P(), P(None, "cols"), P("rows", "cols")),
        check_vma=False,
    )
```

time: 506 us -> 219 us (0.43); the launches traced: 500 us -> 219 us
  waiting for transfers between devices: 333 us -> 0 us
  Pallas kernels: 0 us -> 209 us
  matrix products: 69.9 us -> 0 us
  other arithmetic: 55.6 us -> 0 us
  between operations: 17.4 us -> 0.64 us
  local copies, waits for them, and re-layouts: 24 us -> 9.09 us
    psum x2 -> x0, waiting for transfers between devices: 333 us -> none  [the longest x1 260 us: per_device(): gram = lax.psum(local_gram, ('rows', 'cols'))]
    pallas_call x0 -> x1, Pallas kernels: none -> 209 us  [per_device(): pl.pallas_call(functools.partial(kernel, groups, chunk), out_shape=(jax.S...]
    dot_general x3 -> x0, matrix products: 66.3 us -> none  [product(): jnp.dot(left, right, precision=lax.Precision.HIGHEST, preferred_element_t...]
    another operation x10 -> x0, other arithmetic: 54.6 us -> none  [the longest x6 34 us: per_device(): lower = jnp.linalg.cholesky(gram)]
    unnamed x3, local copies, waits for them, and re-layouts: 18.8 us -> 9.09 us
  transfers between devices with their start and end apart: 3 -> 0, of which waited for: 2 -> 0; matrix products, arithmetic and copies ran while one was open for 14% -> 0% of each run, Pallas kernels for 0% -> 0%
where the time goes in v1:
time: 219 us
  Pallas kernels  209 us (95%)
  local copies, waits for them, and re-layouts  9.09 us (4%)
    pallas_call x1, Pallas kernels, per_device(): pl.pallas_call(functools.partial(kernel, groups, chunk), out_shape=(jax.S...  209 us
    unnamed x3, local copies, waits for them, and re-layouts  9.09 us

profile of v1, /device:TPU:1, one launch (start us, length us, event | category | flops | bytes accessed | tf_op | source)
XLA Modules:
  0.0 218.6 jit_solution(15125595467446684224)
XLA Ops:
  0.6 208.9 %shard_map.49 = (f32[256,256]{1,0:T(8,128)}, f32[256,128]{1,0:T(8,128)}, f32[16384,128]{1,0:T(8,128)}) custom-call(f32[4096,256]{1,0:T(8,128)} %panel.1, f32[16384,128]{1,0:T(8,128)} %trailing.1), custom_call_target="tpu_custom_call" | custom-call | tf_op jit(solution)/shard_map/pallas_call | solution.py:312
  209.5 1.7 copy.8
  211.2 1.6 copy.9
  212.8 5.9 %copy.10 = f32[16384,128]{1,0:T(8,128)} copy(f32[16384,128]{1,0:T(8,128)} %get-tuple-element.8) | data formatting | bytes 16777216

commit v2 on v1

--- a/solution.py
+++ b/solution.py
@@ -60,10 +60,10 @@
 
 def kernel(
     groups, chunk,
-    panel, trailing, r_factor, r_cross, residual,
-    held, trail, high, low, turned, gram, gram_in, gram_y, gram_all, work, both,
+    panel, trailing, r_factor, r_cross, coeff, trail, high, low,
+    held, turned, gram, gram_in, gram_y, gram_all, work, both,
     acc, cross_out, cross_in, cross_all,
-    own_sem, trail_sem, out_sem,
+    own_sem, trail_sem,
     send_r, send_l, recv_l, recv_r, pass_send_r, pass_send_l, pass_recv_l, pass_recv_r,
     small_send, small_recv,
 ):
@@ -71,6 +71,7 @@
     columns = trailing.shape[1]
     own = panel.shape[0] // chunk
     half = own // 2
+    early = max(own * 3 // 8, 1)
     chunks = trailing.shape[0] // chunk
     part = width // groups
     me = lax.axis_index("rows")
@@ -90,11 +91,6 @@
             trailing.at[pl.ds(c * chunk, chunk)], trail.at[c], trail_sem.at[c]
         )
 
-    def store(c):
-        return pltpu.make_async_copy(
-            trail.at[c], residual.at[pl.ds(c * chunk, chunk)], out_sem.at[c]
-        )
-
     loop(own, lambda c: load_panel(c).start())
     loop(chunks, lambda c: load_trail(c).start())
 
@@ -152,7 +148,7 @@
         to_right(c).start()
         to_left(lax.rem(c + half, own)).start()
 
-    loop(own, send_own)
+    loop(early, send_own)
 
     gram[...] = jnp.zeros_like(gram)
     both[...] = jnp.zeros_like(both)
@@ -207,6 +203,7 @@
         return copy_y(gram_y.at[y], gram_y.at[y], small_send.at[1], small_recv.at[1], side(d))
 
     loop(sides - 1, lambda d: over_y(d).start())
+    loop(own - early, lambda c: send_own(early + c))
 
     acc[...] = jnp.zeros_like(acc)
 
@@ -276,28 +273,42 @@
     cross = jnp.concatenate([flat[:columns], flat[columns:]], axis=1)
     solved = exact(both[...], cross, ((1,), (1,)))
     r_cross[...] = solved[:width]
-    c_high, c_low = split(solved[width:])
+    coeff[...] = solved[width:]
+
+    def finish(c):
+        to_right(c).wait_send()
+        to_left(c).wait_send()
+
+    loop(own, finish)
+
+    def finish_passed(c):
+        pass_right(c).wait_send()
+        pass_left(c).wait_send()
+
+    loop(half, finish_passed)
+
+
+def residual_kernel(
+    r_factor_in, r_cross_in, coeff, trail, high, low, r_factor, r_cross, residual, staged, out_sem
+):
+    chunks, chunk, columns = trail.shape
+    c_high, c_low = split(coeff[...])
     c_both = jnp.concatenate([c_high, c_low], axis=1)
+
+    def store(c):
+        return pltpu.make_async_copy(
+            staged.at[c], residual.at[pl.ds(c * chunk, chunk)], out_sem.at[c]
+        )
 
     def project(c):
         product = dot(high[c], c_both)
         rest = product[:, columns:] + dot(low[c], c_high)
-        trail[c] = trail[c] - (product[:, :columns] + rest)
+        staged[c] = trail[c] - (product[:, :columns] + rest)
         store(c).start()
 
     loop(chunks, project)
-
-    def finish(c):
-        to_right(c).wait_send()
-        to_left(c).wait_send()
-
-    loop(own, finish)
-
-    def finish_passed(c):
-        pass_right(c).wait_send()
-        pass_left(c).wait_send()
-
-    loop(half, finish_passed)
+    r_factor[...] = r_factor_in[...]
+    r_cross[...] = r_cross_in[...]
     loop(chunks, lambda c: store(c).wait())
 
 
@@ -309,24 +320,22 @@
     sides = total // rows
     f32, bf16 = jnp.float32, jnp.bfloat16
     dma = pltpu.SemaphoreType.DMA
-    return pl.pallas_call(
+    hbm = pl.BlockSpec(memory_space=pl.ANY)
+    vmem = pl.BlockSpec(memory_space=pltpu.VMEM)
+    r_factor, r_cross, coeff, trail, high, low = pl.pallas_call(
         functools.partial(kernel, groups, chunk),
         out_shape=(
-            jax.ShapeDtypeStruct((width, width), f32),
-            jax.ShapeDtypeStruct((width, columns), f32),
-            jax.ShapeDtypeStruct((total, columns), f32),
-        ),
-        in_specs=[pl.BlockSpec(memory_space=pl.ANY)] * 2,
-        out_specs=(
-            pl.BlockSpec(memory_space=pltpu.VMEM),
-            pl.BlockSpec(memory_space=pltpu.VMEM),
-            pl.BlockSpec(memory_space=pl.ANY),
-        ),
-        scratch_shapes=[
-            pltpu.VMEM((chunks, chunk, width), f32),
+            pltpu.VMEM((width, width), f32),
+            pltpu.VMEM((width, columns), f32),
+            pltpu.VMEM((width, columns), f32),
             pltpu.VMEM((chunks, chunk, columns), f32),
             pltpu.VMEM((chunks, chunk, width), bf16),
             pltpu.VMEM((chunks, chunk, width), bf16),
+        ),
+        in_specs=[hbm] * 2,
+        out_specs=(vmem,) * 6,
+        scratch_shapes=[
+            pltpu.VMEM((chunks, chunk, width), f32),
             pltpu.VMEM((chunks, 2 * columns, chunk), bf16),
             pltpu.VMEM((width, width), f32),
             pltpu.VMEM((groups, part, width), f32),
@@ -338,15 +347,27 @@
             pltpu.VMEM((width, columns), f32),
             pltpu.VMEM((groups, part, columns), f32),
             pltpu.VMEM((groups, part, columns), f32),
-            dma((own,)), dma((chunks,)), dma((chunks,)),
+            dma((own,)), dma((chunks,)),
             dma((own,)), dma((own,)), dma((own,)), dma((own,)),
             dma((half,)), dma((half,)), dma((half,)), dma((half,)),
             dma((5,)), dma((5,)),
         ],
         compiler_params=pltpu.CompilerParams(
-            collective_id=0, has_side_effects=True, vmem_limit_bytes=60 * 2**20
+            collective_id=0, has_side_effects=True, vmem_limit_bytes=30 * 2**20
         ),
     )(panel, trailing)
+    return pl.pallas_call(
+        residual_kernel,
+        out_shape=(
+            jax.ShapeDtypeStruct((width, width), f32),
+            jax.ShapeDtypeStruct((width, columns), f32),
+            jax.ShapeDtypeStruct((total, columns), f32),
+        ),
+        in_specs=[vmem] * 6,
+        out_specs=(vmem, vmem, hbm),
+        scratch_shapes=[pltpu.VMEM((chunks, chunk, columns), f32), dma((chunks,))],
+        compiler_params=pltpu.CompilerParams(vmem_limit_bytes=10 * 2**20),
+    )(r_factor, r_cross, coeff, trail, high, low)
 
 
 def solution(mesh):

time: 219 us -> 172 us (0.79)
  Pallas kernels: 209 us -> 171 us
  local copies, waits for them, and re-layouts: 9.09 us -> 0 us
    pallas_call x1 -> x2, Pallas kernels: 209 us -> 171 us  [the longest x1 160 us: per_device(): pl.pallas_call(functools.partial(kernel, groups, chunk), out_shape=(pltpu...]
    unnamed x3 -> x0, local copies, waits for them, and re-layouts: 9.09 us -> none
where the time goes in v2:
time: 172 us
  Pallas kernels  171 us (99%)
    pallas_call x1, Pallas kernels, per_device(): pl.pallas_call(functools.partial(kernel, groups, chunk), out_shape=(pltpu...  160 us
    pallas_call x1, Pallas kernels, per_device(): pl.pallas_call(residual_kernel, out_shape=(jax.ShapeDtypeStruct((width, w...  11.2 us

profile of v2, /device:TPU:1, one launch (start us, length us, event | category | flops | bytes accessed | tf_op | source)
XLA Modules:
  0.0 171.9 jit_solution(11538400742327705663)
XLA Ops:
  0.6 160.1 %shard_map.49 = (f32[256,256]{1,0:T(8,128)S(1)}, f32[256,128]{1,0:T(8,128)S(1)}, f32[256,128]{1,0:T(8,128)S(1)}, f32[32,512,128]{2,1,0:T(8,128)S(1)}, bf16[32,51...) custom-call(f32[4096,256]{1,0:T(8,128)} %panel.1, f32[16384,128]{1,0:T(8,128)} %trailing.1), custom_call_target="tpu_custom_call" | custom-call | tf_op jit(solution)/shard_map/pallas_call | solution.py:325
  160.7 11.2 %shard_map.50 = (f32[256,256]{1,0:T(8,128)}, f32[256,128]{1,0:T(8,128)}, f32[16384,128]{1,0:T(8,128)}) custom-call(f32[256,256]{1,0:T(8,128)S(1)} %get-tuple-element.9.r_factor_in, f32[256,128]{1,0:T(8,128)S(1)} %get-tuple-element.10.r_cross_in, f32[256,128]{1,0:T(8,128)S(1)} %get-tuple-element.11.coeff, f32[32,512,128]{2,1,0:T(8,128)S(1)} %get-tuple-element.12.trail, ...), custom_call_target="tpu_custom_call" | custom-call | tf_op jit(solution)/shard_map/pallas_call | solution.py:359

commit v3 on v2

--- a/solution.py
+++ b/solution.py
@@ -1,4 +1,5 @@
 import functools
+import math
 
 import jax
 import jax.numpy as jnp
@@ -18,6 +19,10 @@
 
 def dot(a, b):
     return jnp.dot(a, b, preferred_element_type=jnp.float32)
+
+
+def dot_turned(a, b):
+    return lax.dot_general(a, b, (((1,), (1,)), ((), ())), preferred_element_type=jnp.float32)
 
 
 def exact(a, b, dims):
@@ -59,13 +64,13 @@
 
 
 def kernel(
-    groups, chunk,
+    groups, ring, chunk,
     panel, trailing, r_factor, r_cross, coeff, trail, high, low,
-    held, turned, gram, gram_in, gram_y, gram_all, work, both,
+    held, turned, gram, gram_in, gram_y, gram_all, work, both, both_high, both_low,
     acc, cross_out, cross_in, cross_all,
     own_sem, trail_sem,
     send_r, send_l, recv_l, recv_r, pass_send_r, pass_send_l, pass_recv_l, pass_recv_r,
-    small_send, small_recv,
+    small_send, small_recv, news,
 ):
     width = panel.shape[1]
     columns = trailing.shape[1]
@@ -94,18 +99,46 @@
     loop(own, lambda c: load_panel(c).start())
     loop(chunks, lambda c: load_trail(c).start())
 
-    def peer(d):
-        return lax.rem(me + d + 1, groups)
+    core, z, x = lax.rem(me, 2), lax.rem(me // 2, ring), me // (2 * ring)
+
+    def at_xz(dx, dz, other):
+        return (lax.rem(x + dx, ring) * ring + lax.rem(z + dz, ring)) * 2 + lax.rem(core + other, 2)
+
+    def peer(i):
+        return at_xz(ring // 2 + i // (2 * ring), ring // 2 + lax.rem(i // 2, ring), lax.rem(i, 2))
+
+    itself = (ring - ring // 2) * (2 * ring + 2)
+
+    def each_peer(body):
+        loop(itself, lambda i: body(peer(i)))
+        loop(groups - 1 - itself, lambda i: body(peer(itself + 1 + i)))
 
     def side(d):
         return lax.rem(y + d + 1, sides)
 
+    def tell(sem, **to):
+        pl.semaphore_signal(sem, inc=1, device_id=to, device_id_type=MESH)
+
+    def tell_x(sem):
+        tell(sem, rows=at_xz(1, 0, 0))
+        tell(sem, rows=at_xz(ring - 1, 0, 0))
+
+    def tell_y(sem):
+        tell(sem, cols=right)
+        tell(sem, cols=left)
+
+    def tell_z(sem):
+        tell(sem, rows=at_xz(0, 1, 0))
+        tell(sem, rows=at_xz(0, ring - 1, 0))
+
     barrier = pltpu.get_barrier_semaphore()
-    loop(sides - 1, lambda d: pl.semaphore_signal(
-        barrier, inc=1, device_id={"cols": side(d)}, device_id_type=MESH))
-    loop(groups - 1, lambda d: pl.semaphore_signal(
-        barrier, inc=1, device_id={"rows": peer(d)}, device_id_type=MESH))
-    pl.semaphore_wait(barrier, groups + sides - 2)
+    tell_y(barrier)
+    tell_x(barrier)
+    tell_z(barrier)
+    tell(barrier, rows=at_xz(0, 0, 1))
+    pl.semaphore_wait(barrier, 7)
+    tell_x(news.at[0])
+    tell_y(news.at[1])
 
     def copy_y(src, dst, send, recv, to):
         return pltpu.make_async_remote_copy(
@@ -165,29 +198,27 @@
         both[:width, :] += dot(x_turned, x_low)
 
     loop(own, gram_step)
+    pl.semaphore_wait(news.at[0], 2)
+    tell_z(news.at[2])
     mixed = both[:width, :]
     gram[...] += mixed + mixed.T
 
     def spread(src_of, dst, stage):
-        def one(d):
-            to = peer(d)
+        def one(to):
             pltpu.make_async_remote_copy(
                 src_ref=src_of(to), dst_ref=dst.at[me],
                 send_sem=small_send.at[stage], recv_sem=small_recv.at[stage],
                 device_id={"rows": to}, device_id_type=MESH).start()
 
-        loop(groups - 1, one)
+        each_peer(one)
 
     def spread_wait(dst, stage):
         some = dst.at[pl.ds(0, groups - 1)]
         everything = pltpu.make_async_remote_copy(
             src_ref=some, dst_ref=some,
             send_sem=small_send.at[stage], recv_sem=small_recv.at[stage],
-            device_id={"rows": peer(0)}, device_id_type=MESH)
+            device_id={"rows": at_xz(1, 0, 0)}, device_id_type=MESH)
         everything.wait()
-
-    spread(lambda to: gram.at[pl.ds(pl.multiple_of(to * part, 8), part)], gram_in, 0)
-    gram_in[me] = gram[pl.ds(pl.multiple_of(me * part, 8), part), :]
 
     def turn(c):
         load_trail(c).wait()
@@ -195,7 +226,20 @@
         turned[c, :columns, :] = t_high
         turned[c, columns:, :] = t_low
 
-    loop(chunks, turn)
+    third = chunks // 3
+    loop(third, turn)
+    pl.semaphore_wait(news.at[2], 2)
+    tell_z(news.at[3])
+    loop(third, lambda c: turn(third + c))
+    pl.semaphore_wait(news.at[3], 2)
+    tell(news.at[4], rows=at_xz(0, 0, 1))
+    loop(chunks - 2 * third, lambda c: turn(2 * third + c))
+    pl.semaphore_wait(news.at[4], 1)
+    pl.semaphore_wait(news.at[1], 2)
+
+    spread(lambda to: gram.at[pl.ds(pl.multiple_of(to * part, 8), part)], gram_in, 0)
+    gram_in[me] = gram[pl.ds(pl.multiple_of(me * part, 8), part), :]
+
     spread_wait(gram_in, 0)
     gram_y[y] = jnp.sum(gram_in[...], axis=0)
 
@@ -229,6 +273,7 @@
     inverse = work[:, width:]
     both[:width, :] = inverse
     both[width:, :] = exact(inverse, inverse, ((0,), (0,)))
+    both_high[...], both_low[...] = split(both[...])
 
     def take(at):
         x_high, x_low = split(held[at])
@@ -271,7 +316,10 @@
 
     flat = cross_all[...].reshape(width, columns)
     cross = jnp.concatenate([flat[:columns], flat[columns:]], axis=1)
-    solved = exact(both[...], cross, ((1,), (1,)))
+    x_high, x_low = split(cross)
+    product = dot_turned(both_high[...], jnp.concatenate([x_high, x_low], axis=0))
+    rest = product[:, columns:] + dot_turned(both_low[...], x_high)
+    solved = product[:, :columns] + rest
     r_cross[...] = solved[:width]
     coeff[...] = solved[width:]
 
@@ -295,24 +343,28 @@
     c_high, c_low = split(coeff[...])
     c_both = jnp.concatenate([c_high, c_low], axis=1)
 
+    steps, rows = chunks // 2, 2 * chunk
+
     def store(c):
         return pltpu.make_async_copy(
-            staged.at[c], residual.at[pl.ds(c * chunk, chunk)], out_sem.at[c]
+            staged.at[c], residual.at[pl.ds(c * rows, rows)], out_sem.at[c]
         )
 
-    def project(c):
-        product = dot(high[c], c_both)
-        rest = product[:, columns:] + dot(low[c], c_high)
-        staged[c] = trail[c] - (product[:, :columns] + rest)
+    def some(ref, c):
+        return ref[2 * c : 2 * c + 2].reshape(rows, ref.shape[2])
+
+    for c in range(steps):
+        product = dot(some(high, c), c_both)
+        rest = product[:, columns:] + dot(some(low, c), c_high)
+        staged[c] = some(trail, c) - (product[:, :columns] + rest)
         store(c).start()
-
-    loop(chunks, project)
     r_factor[...] = r_factor_in[...]
     r_cross[...] = r_cross_in[...]
-    loop(chunks, lambda c: store(c).wait())
+    loop(steps, lambda c: store(c).wait())
 
 
 def per_device(groups, chunk, panel, trailing):
+    ring = math.isqrt(groups // 2)
     rows, width = panel.shape
     total, columns = trailing.shape
     own, chunks, part = rows // chunk, total // chunk, width // groups
@@ -323,7 +375,7 @@
     hbm = pl.BlockSpec(memory_space=pl.ANY)
     vmem = pl.BlockSpec(memory_space=pltpu.VMEM)
     r_factor, r_cross, coeff, trail, high, low = pl.pallas_call(
-        functools.partial(kernel, groups, chunk),
+        functools.partial(kernel, groups, ring, chunk),
         out_shape=(
             pltpu.VMEM((width, width), f32),
             pltpu.VMEM((width, columns), f32),
@@ -343,6 +395,8 @@
             pltpu.VMEM((groups, part, width), f32),
             pltpu.VMEM((width, 2 * width), f32),
             pltpu.VMEM((2 * width, width), f32),
+            pltpu.VMEM((2 * width, width), bf16),
+            pltpu.VMEM((2 * width, width), bf16),
             pltpu.VMEM((columns, width), f32),
             pltpu.VMEM((width, columns), f32),
             pltpu.VMEM((groups, part, columns), f32),
@@ -350,7 +404,7 @@
             dma((own,)), dma((chunks,)),
             dma((own,)), dma((own,)), dma((own,)), dma((own,)),
             dma((half,)), dma((half,)), dma((half,)), dma((half,)),
-            dma((5,)), dma((5,)),
+            dma((5,)), dma((5,)), pltpu.SemaphoreType.REGULAR((5,)),
         ],
         compiler_params=pltpu.CompilerParams(
             collective_id=0, has_side_effects=True, vmem_limit_bytes=30 * 2**20
@@ -365,7 +419,7 @@
         ),
         in_specs=[vmem] * 6,
         out_specs=(vmem, vmem, hbm),
-        scratch_shapes=[pltpu.VMEM((chunks, chunk, columns), f32), dma((chunks,))],
+        scratch_shapes=[pltpu.VMEM((chunks // 2, 2 * chunk, columns), f32), dma((chunks // 2,))],
         compiler_params=pltpu.CompilerParams(vmem_limit_bytes=10 * 2**20),
     )(r_factor, r_cross, coeff, trail, high, low)
 

time: 172 us -> 164 us (0.953)
  Pallas kernels: 171 us -> 163 us
    pallas_call x1, Pallas kernels: 11.2 us -> 6.22 us  [per_device(): pl.pallas_call(residual_kernel, out_shape=(jax.ShapeDtypeStruct((width, w...]
    pallas_call x1, Pallas kernels: 160 us -> 157 us  [per_device(): pl.pallas_call(functools.partial(kernel, groups, ring, chunk), out_shape=...]
where the time goes in v3:
time: 164 us
  Pallas kernels  163 us (99%)
    pallas_call x1, Pallas kernels, per_device(): pl.pallas_call(functools.partial(kernel, groups, ring, chunk), out_shape=...  157 us
    pallas_call x1, Pallas kernels, per_device(): pl.pallas_call(residual_kernel, out_shape=(jax.ShapeDtypeStruct((width, w...  6.22 us

profile of v3, /device:TPU:1, one launch (start us, length us, event | category | flops | bytes accessed | tf_op | source)
XLA Modules:
  0.0 164.0 jit_solution(1148744713360994983)
XLA Ops:
  0.6 157.1 %shard_map.49 = (f32[256,256]{1,0:T(8,128)S(1)}, f32[256,128]{1,0:T(8,128)S(1)}, f32[256,128]{1,0:T(8,128)S(1)}, f32[32,512,128]{2,1,0:T(8,128)S(1)}, bf16[32,51...) custom-call(f32[4096,256]{1,0:T(8,128)} %panel.1, f32[16384,128]{1,0:T(8,128)} %trailing.1), custom_call_target="tpu_custom_call" | custom-call | tf_op jit(solution)/shard_map/pallas_call | solution.py:377
  157.7 6.2 %shard_map.50 = (f32[256,256]{1,0:T(8,128)}, f32[256,128]{1,0:T(8,128)}, f32[16384,128]{1,0:T(8,128)}) custom-call(f32[256,256]{1,0:T(8,128)S(1)} %get-tuple-element.9.r_factor_in, f32[256,128]{1,0:T(8,128)S(1)} %get-tuple-element.10.r_cross_in, f32[256,128]{1,0:T(8,128)S(1)} %get-tuple-element.11.coeff, f32[32,512,128]{2,1,0:T(8,128)S(1)} %get-tuple-element.12.trail, ...), custom_call_target="tpu_custom_call" | custom-call | tf_op jit(solution)/shard_map/pallas_call | solution.py:413

commit v4 on v3

--- a/solution.py
+++ b/solution.py
@@ -9,6 +9,9 @@
 from jax.sharding import PartitionSpec as P
 
 MESH = pl.DeviceIdType.MESH
+CHUNK = 512
+LATE = 1
+STEPS = 16
 BLOCK = 32
 
 
@@ -64,13 +67,13 @@
 
 
 def kernel(
-    groups, ring, chunk,
+    groups, ring, chunk, late,
     panel, trailing, r_factor, r_cross, coeff, trail, high, low,
     held, turned, gram, gram_in, gram_y, gram_all, work, both, both_high, both_low,
-    acc, cross_out, cross_in, cross_all,
+    acc, cross_out, cross_in, cross_all, guest, guest_out, guest_in, guest_sum, guest_part,
     own_sem, trail_sem,
     send_r, send_l, recv_l, recv_r, pass_send_r, pass_send_l, pass_recv_l, pass_recv_r,
-    small_send, small_recv, news,
+    small_send, small_recv, guest_send, guest_recv, part_send, part_recv, news,
 ):
     width = panel.shape[1]
     columns = trailing.shape[1]
@@ -177,6 +180,20 @@
         return copy_y(held.at[across * own + half + c], held.at[across * own + half + c],
                       pass_send_l.at[c], pass_recv_r.at[c], left)
 
+    def guest_left():
+        rows = trailing.at[pl.ds((across * own + half - late) * chunk, late * chunk)]
+        return copy_y(rows, guest.at[0], guest_send.at[0], guest_recv.at[0], left)
+
+    def guest_right():
+        rows = trailing.at[pl.ds((across * own + own - late) * chunk, late * chunk)]
+        return copy_y(rows, guest.at[1], guest_send.at[1], guest_recv.at[1], right)
+
+    def part_right():
+        return copy_y(guest_sum.at[0], guest_part.at[0], part_send.at[0], part_recv.at[0], right)
+
+    def part_left():
+        return copy_y(guest_sum.at[1], guest_part.at[1], part_send.at[1], part_recv.at[1], left)
+
     def send_own(c):
         to_right(c).start()
         to_left(lax.rem(c + half, own)).start()
@@ -247,14 +264,32 @@
         return copy_y(gram_y.at[y], gram_y.at[y], small_send.at[1], small_recv.at[1], side(d))
 
     loop(sides - 1, lambda d: over_y(d).start())
+    guest_left().start()
+    guest_right().start()
     loop(own - early, lambda c: send_own(early + c))
 
     acc[...] = jnp.zeros_like(acc)
 
+    def cross_of(t_both, at):
+        x_high, x_low = (
+            ref[pl.ds(at, t_both.shape[1] // chunk)].reshape(t_both.shape[1], width)
+            for ref in (high, low))
+        product = dot(t_both, x_high)
+        return product[:columns] + (product[columns:] + dot(t_both[:columns], x_low))
+
     def add_cross(at):
-        product = dot(turned[at], high[at])
-        acc[...] += product[:columns] + (
-            product[columns:] + dot(turned[at, :columns, :], low[at]))
+        acc[...] += cross_of(turned[at], at)
+
+    def lay(out, first, sums):
+        for side_at in range(width // 128):
+            out[pl.ds(side_at * columns, columns), first : first + columns] = (
+                sums[:, side_at * 128 : side_at * 128 + 128])
+
+    def mine(ref):
+        return ref[pl.ds(pl.multiple_of(me * part, 8), part), :]
+
+    def slice_for(ref):
+        return lambda to: ref.at[pl.ds(pl.multiple_of(to * part, 8), part)]
 
     loop(own, lambda c: add_cross(y * own + c))
 
@@ -289,6 +324,20 @@
         take(left * own + c)
         take(right * own + half + c)
 
+    def guests():
+        for c in range(half - late, half):
+            from_left(c).wait_recv()
+            take(left * own + c)
+            from_right(half + c).wait_recv()
+            take(right * own + half + c)
+        for place, at in ((0, left * own + half - late), (1, right * own + own - late)):
+            copy_y(guest.at[place], guest.at[place],
+                   guest_send.at[place], guest_recv.at[place], right).wait_recv()
+            t_both = jnp.concatenate(split(guest[place].T), axis=0)
+            lay(guest_out, place * columns, cross_of(t_both, at))
+        spread(slice_for(guest_out), guest_in, 5)
+        guest_in[me] = mine(guest_out)
+
     def second_half(c):
         from_left(half + c).wait_recv()
         take(left * own + half + c)
@@ -301,16 +350,28 @@
         passed_right(c).wait_recv()
         take(across * own + half + c)
 
-    loop(half, first_half)
+    loop(half - late, first_half)
+    guests()
     loop(half, second_half)
-    loop(half, passed)
-
-    for side_at in range(width // 128):
-        cross_out[pl.ds(side_at * columns, columns), :] = acc[:, side_at * 128 : side_at * 128 + 128]
-    spread(lambda to: cross_out.at[pl.ds(pl.multiple_of(to * part, 8), part)], cross_in, 3)
-    cross_in[me] = cross_out[pl.ds(pl.multiple_of(me * part, 8), part), :]
+    spread_wait(guest_in, 5)
+    sums = jnp.sum(guest_in[...], axis=0)
+    guest_sum[0] = sums[:, :columns]
+    guest_sum[1] = sums[:, columns:]
+    part_right().start()
+    part_left().start()
+    for c in range(half - late, half):
+        pass_right(c).start()
+        pass_left(c).start()
+    loop(half - late, passed)
+
+    lay(cross_out, 0, acc[...])
+    spread(slice_for(cross_out), cross_in, 3)
+    cross_in[me] = mine(cross_out)
+    for place in range(2):
+        copy_y(guest_part.at[place], guest_part.at[place],
+               part_send.at[place], part_recv.at[place], right).wait_recv()
     spread_wait(cross_in, 3)
-    cross_all[me] = jnp.sum(cross_in[...], axis=0)
+    cross_all[me] = jnp.sum(cross_in[...], axis=0) + (guest_part[0] + guest_part[1])
     spread(lambda to: cross_all.at[me], cross_all, 4)
     spread_wait(cross_all, 4)
 
@@ -323,6 +384,15 @@
     r_cross[...] = solved[:width]
     coeff[...] = solved[width:]
 
+    def keep(at):
+        high[at], low[at] = split(held[at])
+
+    for c in range(half - late, half):
+        passed_left(c).wait_recv()
+        keep(across * own + c)
+        passed_right(c).wait_recv()
+        keep(across * own + half + c)
+
     def finish(c):
         to_right(c).wait_send()
         to_left(c).wait_send()
@@ -334,6 +404,8 @@
         pass_left(c).wait_send()
 
     loop(half, finish_passed)
+    for copy in (guest_left(), guest_right(), part_right(), part_left()):
+        copy.wait_send()
 
 
 def residual_kernel(
@@ -343,7 +415,8 @@
     c_high, c_low = split(coeff[...])
     c_both = jnp.concatenate([c_high, c_low], axis=1)
 
-    steps, rows = chunks // 2, 2 * chunk
+    steps, rows = STEPS, chunks * chunk // STEPS
+    each = chunks // steps
 
     def store(c):
         return pltpu.make_async_copy(
@@ -351,7 +424,7 @@
         )
 
     def some(ref, c):
-        return ref[2 * c : 2 * c + 2].reshape(rows, ref.shape[2])
+        return ref[each * c : each * (c + 1)].reshape(rows, ref.shape[2])
 
     for c in range(steps):
         product = dot(some(high, c), c_both)
@@ -363,7 +436,7 @@
     loop(steps, lambda c: store(c).wait())
 
 
-def per_device(groups, chunk, panel, trailing):
+def per_device(groups, chunk, late, panel, trailing):
     ring = math.isqrt(groups // 2)
     rows, width = panel.shape
     total, columns = trailing.shape
@@ -375,7 +448,7 @@
     hbm = pl.BlockSpec(memory_space=pl.ANY)
     vmem = pl.BlockSpec(memory_space=pltpu.VMEM)
     r_factor, r_cross, coeff, trail, high, low = pl.pallas_call(
-        functools.partial(kernel, groups, ring, chunk),
+        functools.partial(kernel, groups, ring, chunk, late),
         out_shape=(
             pltpu.VMEM((width, width), f32),
             pltpu.VMEM((width, columns), f32),
@@ -401,10 +474,15 @@
             pltpu.VMEM((width, columns), f32),
             pltpu.VMEM((groups, part, columns), f32),
             pltpu.VMEM((groups, part, columns), f32),
+            pltpu.VMEM((2, late * chunk, columns), f32),
+            pltpu.VMEM((width, 2 * columns), f32),
+            pltpu.VMEM((groups, part, 2 * columns), f32),
+            pltpu.VMEM((2, part, columns), f32),
+            pltpu.VMEM((2, part, columns), f32),
             dma((own,)), dma((chunks,)),
             dma((own,)), dma((own,)), dma((own,)), dma((own,)),
             dma((half,)), dma((half,)), dma((half,)), dma((half,)),
-            dma((5,)), dma((5,)), pltpu.SemaphoreType.REGULAR((5,)),
+            dma((6,)), dma((6,)), dma((2,)), dma((2,)), dma((2,)), dma((2,)), pltpu.SemaphoreType.REGULAR((5,)),
         ],
         compiler_params=pltpu.CompilerParams(
             collective_id=0, has_side_effects=True, vmem_limit_bytes=30 * 2**20
@@ -419,14 +497,14 @@
         ),
         in_specs=[vmem] * 6,
         out_specs=(vmem, vmem, hbm),
-        scratch_shapes=[pltpu.VMEM((chunks // 2, 2 * chunk, columns), f32), dma((chunks // 2,))],
+        scratch_shapes=[pltpu.VMEM((STEPS, total // STEPS, columns), f32), dma((STEPS,))],
         compiler_params=pltpu.CompilerParams(vmem_limit_bytes=10 * 2**20),
     )(r_factor, r_cross, coeff, trail, high, low)
 
 
 def solution(mesh):
     return jax.shard_map(
-        functools.partial(per_device, mesh.shape["rows"], 512),
+        functools.partial(per_device, mesh.shape["rows"], CHUNK, LATE),
         mesh=mesh,
         in_specs=(P(("rows", "cols"), None), P("rows", "cols")),
         out_specs=(P(), P(None, "cols"), P("rows", "cols")),

time: 164 us -> 160 us (0.976)
  Pallas kernels: 163 us -> 159 us
    pallas_call x1, Pallas kernels: 157 us -> 153 us  [per_device(): pl.pallas_call(functools.partial(kernel, groups, ring, chunk, late), out_...]
where the time goes in v4:
time: 160 us
  Pallas kernels  159 us (99%)
    pallas_call x1, Pallas kernels, per_device(): pl.pallas_call(functools.partial(kernel, groups, ring, chunk, late), out_...  153 us
    pallas_call x1, Pallas kernels, per_device(): pl.pallas_call(residual_kernel, out_shape=(jax.ShapeDtypeStruct((width, w...  6.22 us

profile of v4, /device:TPU:1, one launch (start us, length us, event | category | flops | bytes accessed | tf_op | source)
XLA Modules:
  0.0 159.8 jit_solution(2304196737193271293)
XLA Ops:
  0.6 152.9 %shard_map.49 = (f32[256,256]{1,0:T(8,128)S(1)}, f32[256,128]{1,0:T(8,128)S(1)}, f32[256,128]{1,0:T(8,128)S(1)}, f32[32,512,128]{2,1,0:T(8,128)S(1)}, bf16[32,51...) custom-call(f32[4096,256]{1,0:T(8,128)} %panel.1, f32[16384,128]{1,0:T(8,128)} %trailing.1), custom_call_target="tpu_custom_call" | custom-call | tf_op jit(solution)/shard_map/pallas_call | solution.py:450
  153.5 6.2 %shard_map.50 = (f32[256,256]{1,0:T(8,128)}, f32[256,128]{1,0:T(8,128)}, f32[16384,128]{1,0:T(8,128)}) custom-call(f32[256,256]{1,0:T(8,128)S(1)} %get-tuple-element.9.r_factor_in, f32[256,128]{1,0:T(8,128)S(1)} %get-tuple-element.10.r_cross_in, f32[256,128]{1,0:T(8,128)S(1)} %get-tuple-element.11.coeff, f32[32,512,128]{2,1,0:T(8,128)S(1)} %get-tuple-element.12.trail, ...), custom_call_target="tpu_custom_call" | custom-call | tf_op jit(solution)/shard_map/pallas_call | solution.py:491

commit v5 on v4

--- a/solution.py
+++ b/solution.py
@@ -9,8 +9,8 @@
 from jax.sharding import PartitionSpec as P
 
 MESH = pl.DeviceIdType.MESH
-CHUNK = 512
-LATE = 1
+CHUNK = 256
+LATE = 3
 STEPS = 16
 BLOCK = 32
 
@@ -40,6 +40,28 @@
         return carry
 
     lax.fori_loop(0, n, step, 0)
+
+
+def split_coeff(coeff):
+    high, low = split(coeff)
+    return high, jnp.concatenate([high, low], axis=1)
+
+
+def project(weights, trail, high, low, c):
+    chunks, chunk, columns = trail.shape
+    each = chunks // STEPS
+
+    def some(ref):
+        return ref[each * c : each * (c + 1)].reshape(each * chunk, ref.shape[2])
+
+    c_high, c_both = weights
+    product = dot(some(high), c_both)
+    rest = product[:, columns:] + dot(some(low), c_high)
+    return (some(trail) - (product[:, :columns] + rest)).reshape(each, chunk, columns)
+
+
+def whole(c):
+    return c % 2 == 0
 
 
 def factor(work, width):
@@ -99,9 +121,6 @@
             trailing.at[pl.ds(c * chunk, chunk)], trail.at[c], trail_sem.at[c]
         )
 
-    loop(own, lambda c: load_panel(c).start())
-    loop(chunks, lambda c: load_trail(c).start())
-
     core, z, x = lax.rem(me, 2), lax.rem(me // 2, ring), me // (2 * ring)
 
     def at_xz(dx, dz, other):
@@ -139,6 +158,7 @@
     tell_x(barrier)
     tell_z(barrier)
     tell(barrier, rows=at_xz(0, 0, 1))
+    loop(own, lambda c: load_panel(c).start())
     pl.semaphore_wait(barrier, 7)
     tell_x(news.at[0])
     tell_y(news.at[1])
@@ -199,6 +219,7 @@
         to_left(lax.rem(c + half, own)).start()
 
     loop(early, send_own)
+    loop(chunks, lambda c: load_trail(c).start())
 
     gram[...] = jnp.zeros_like(gram)
     both[...] = jnp.zeros_like(both)
@@ -362,6 +383,14 @@
     for c in range(half - late, half):
         pass_right(c).start()
         pass_left(c).start()
+
+    def finish(c):
+        to_right(c).wait_send()
+        to_left(c).wait_send()
+
+    loop(own, finish)
+    for copy in (guest_left(), guest_right()):
+        copy.wait_send()
     loop(half - late, passed)
 
     lay(cross_out, 0, acc[...])
@@ -373,6 +402,14 @@
     spread_wait(cross_in, 3)
     cross_all[me] = jnp.sum(cross_in[...], axis=0) + (guest_part[0] + guest_part[1])
     spread(lambda to: cross_all.at[me], cross_all, 4)
+
+    def finish_passed(c):
+        pass_right(c).wait_send()
+        pass_left(c).wait_send()
+
+    loop(half - late, finish_passed)
+    for copy in (part_right(), part_left()):
+        copy.wait_send()
     spread_wait(cross_all, 4)
 
     flat = cross_all[...].reshape(width, columns)
@@ -383,6 +420,11 @@
     solved = product[:, :columns] + rest
     r_cross[...] = solved[:width]
     coeff[...] = solved[width:]
+    weights = split_coeff(solved[width:])
+    each = chunks // STEPS
+    for c in range(STEPS):
+        if whole(c):
+            trail[each * c : each * (c + 1)] = project(weights, trail, high, low, c)
 
     def keep(at):
         high[at], low[at] = split(held[at])
@@ -393,47 +435,34 @@
         passed_right(c).wait_recv()
         keep(across * own + half + c)
 
-    def finish(c):
-        to_right(c).wait_send()
-        to_left(c).wait_send()
-
-    loop(own, finish)
-
-    def finish_passed(c):
-        pass_right(c).wait_send()
-        pass_left(c).wait_send()
-
-    loop(half, finish_passed)
-    for copy in (guest_left(), guest_right(), part_right(), part_left()):
-        copy.wait_send()
+    loop(late, lambda c: finish_passed(half - late + c))
 
 
 def residual_kernel(
     r_factor_in, r_cross_in, coeff, trail, high, low, r_factor, r_cross, residual, staged, out_sem
 ):
-    chunks, chunk, columns = trail.shape
-    c_high, c_low = split(coeff[...])
-    c_both = jnp.concatenate([c_high, c_low], axis=1)
-
-    steps, rows = STEPS, chunks * chunk // STEPS
-    each = chunks // steps
-
-    def store(c):
+    each = trail.shape[0] // STEPS
+
+    def store(c, rows):
         return pltpu.make_async_copy(
-            staged.at[c], residual.at[pl.ds(c * rows, rows)], out_sem.at[c]
+            rows, residual.at[pl.ds(each * c, each)], out_sem.at[c]
         )
 
-    def some(ref, c):
-        return ref[each * c : each * (c + 1)].reshape(rows, ref.shape[2])
-
-    for c in range(steps):
-        product = dot(some(high, c), c_both)
-        rest = product[:, columns:] + dot(some(low, c), c_high)
-        staged[c] = some(trail, c) - (product[:, :columns] + rest)
-        store(c).start()
+    def rows_of(c):
+        return trail.at[pl.ds(each * c, each)] if whole(c) else staged.at[c // 2]
+
+    for c in range(STEPS):
+        if whole(c):
+            store(c, rows_of(c)).start()
+    weights = split_coeff(coeff[...])
+    for c in range(STEPS):
+        if not whole(c):
+            staged[c // 2] = project(weights, trail, high, low, c)
+            store(c, rows_of(c)).start()
     r_factor[...] = r_factor_in[...]
     r_cross[...] = r_cross_in[...]
-    loop(steps, lambda c: store(c).wait())
+    for c in range(STEPS):
+        store(c, rows_of(c)).wait()
 
 
 def per_device(groups, chunk, late, panel, trailing):
@@ -488,18 +517,19 @@
             collective_id=0, has_side_effects=True, vmem_limit_bytes=30 * 2**20
         ),
     )(panel, trailing)
-    return pl.pallas_call(
+    r_factor, r_cross, residual = pl.pallas_call(
         residual_kernel,
         out_shape=(
             jax.ShapeDtypeStruct((width, width), f32),
             jax.ShapeDtypeStruct((width, columns), f32),
-            jax.ShapeDtypeStruct((total, columns), f32),
+            jax.ShapeDtypeStruct((chunks, chunk, columns), f32),
         ),
         in_specs=[vmem] * 6,
         out_specs=(vmem, vmem, hbm),
-        scratch_shapes=[pltpu.VMEM((STEPS, total // STEPS, columns), f32), dma((STEPS,))],
+        scratch_shapes=[pltpu.VMEM((STEPS // 2, chunks // STEPS, chunk, columns), f32), dma((STEPS,))],
         compiler_params=pltpu.CompilerParams(vmem_limit_bytes=10 * 2**20),
     )(r_factor, r_cross, coeff, trail, high, low)
+    return r_factor, r_cross, residual.reshape(total, columns)
 
 
 def solution(mesh):

time: 160 us -> 159 us (level)
    pallas_call x1, Pallas kernels: 6.22 us -> 4.28 us  [per_device(): pl.pallas_call(residual_kernel, out_shape=(jax.ShapeDtypeStruct((width, w...]
where the time goes in v5:
time: 159 us; the launch traced here: 158 us
  Pallas kernels  158 us (99%)
    pallas_call x1, Pallas kernels, per_device(): pl.pallas_call(functools.partial(kernel, groups, ring, chunk, late), out_...  153 us
    pallas_call x1, Pallas kernels, per_device(): pl.pallas_call(residual_kernel, out_shape=(jax.ShapeDtypeStruct((width, w...  4.28 us

profile of v5, /device:TPU:1, one launch (start us, length us, event | category | flops | bytes accessed | tf_op | source)
XLA Modules:
  0.0 158.3 jit_solution(15542342288576398781)
XLA Ops:
  0.6 153.4 %shard_map.49 = (f32[256,256]{1,0:T(8,128)S(1)}, f32[256,128]{1,0:T(8,128)S(1)}, f32[256,128]{1,0:T(8,128)S(1)}, f32[64,256,128]{2,1,0:T(8,128)S(1)}, bf16[64,25...) custom-call(f32[4096,256]{1,0:T(8,128)} %panel.1, f32[16384,128]{1,0:T(8,128)} %trailing.1), custom_call_target="tpu_custom_call" | custom-call | tf_op jit(solution)/shard_map/pallas_call | solution.py:479
  154.0 4.3 %shard_map.50 = (f32[256,256]{1,0:T(8,128)}, f32[256,128]{1,0:T(8,128)}, f32[64,256,128]{2,1,0:T(8,128)}) custom-call(f32[256,256]{1,0:T(8,128)S(1)} %get-tuple-element.12.r_factor_in, f32[256,128]{1,0:T(8,128)S(1)} %get-tuple-element.13.r_cross_in, f32[256,128]{1,0:T(8,128)S(1)} %get-tuple-element.14.coeff, f32[64,256,128]{2,1,0:T(8,128)S(1)} %get-tuple-element.15.trail, ...), custom_call_target="tpu_custom_call" | custom-call | tf_op jit(solution)/shard_map/pallas_call | solution.py:520

commit v6 on v5

--- a/solution.py
+++ b/solution.py
@@ -9,8 +9,8 @@
 from jax.sharding import PartitionSpec as P
 
 MESH = pl.DeviceIdType.MESH
-CHUNK = 256
-LATE = 3
+CHUNK = 512
+LATE = 1
 STEPS = 16
 BLOCK = 32
 
@@ -104,6 +104,8 @@
     early = max(own * 3 // 8, 1)
     chunks = trailing.shape[0] // chunk
     part = width // groups
+    edge, cut = half - late - 1, chunk // 2
+    late_rows = late * chunk + cut
     me = lax.axis_index("rows")
     y = lax.axis_index("cols")
     sides = trailing.shape[0] // panel.shape[0]
@@ -184,28 +186,31 @@
         return copy_y(held.at[right * own + c], held.at[right * own + c],
                       send_l.at[c], recv_r.at[c], left)
 
-    def pass_right(c):
-        return copy_y(held.at[left * own + c], held.at[left * own + c],
-                      pass_send_r.at[c], pass_recv_l.at[c], right)
-
-    def pass_left(c):
-        return copy_y(held.at[right * own + half + c], held.at[right * own + half + c],
-                      pass_send_l.at[c], pass_recv_r.at[c], left)
-
-    def passed_left(c):
-        return copy_y(held.at[across * own + c], held.at[across * own + c],
-                      pass_send_r.at[c], pass_recv_l.at[c], right)
-
-    def passed_right(c):
-        return copy_y(held.at[across * own + half + c], held.at[across * own + half + c],
-                      pass_send_l.at[c], pass_recv_r.at[c], left)
+    def piece(at, c, rows):
+        return held.at[at + c] if rows is None else held.at[at + c, pl.ds(rows * cut, cut)]
+
+    def pass_right(c, rows=None):
+        ref, sem = piece(left * own, c, rows), half if rows == 1 else c
+        return copy_y(ref, ref, pass_send_r.at[sem], pass_recv_l.at[sem], right)
+
+    def pass_left(c, rows=None):
+        ref, sem = piece(right * own + half, c, rows), half if rows == 1 else c
+        return copy_y(ref, ref, pass_send_l.at[sem], pass_recv_r.at[sem], left)
+
+    def passed_left(c, rows=None):
+        ref, sem = piece(across * own, c, rows), half if rows == 1 else c
+        return copy_y(ref, ref, pass_send_r.at[sem], pass_recv_l.at[sem], right)
+
+    def passed_right(c, rows=None):
+        ref, sem = piece(across * own + half, c, rows), half if rows == 1 else c
+        return copy_y(ref, ref, pass_send_l.at[sem], pass_recv_r.at[sem], left)
 
     def guest_left():
-        rows = trailing.at[pl.ds((across * own + half - late) * chunk, late * chunk)]
+        rows = trailing.at[pl.ds((across * own + half) * chunk - late_rows, late_rows)]
         return copy_y(rows, guest.at[0], guest_send.at[0], guest_recv.at[0], left)
 
     def guest_right():
-        rows = trailing.at[pl.ds((across * own + own - late) * chunk, late * chunk)]
+        rows = trailing.at[pl.ds((across * own + own) * chunk - late_rows, late_rows)]
         return copy_y(rows, guest.at[1], guest_send.at[1], guest_recv.at[1], right)
 
     def part_right():
@@ -291,15 +296,12 @@
 
     acc[...] = jnp.zeros_like(acc)
 
-    def cross_of(t_both, at):
-        x_high, x_low = (
-            ref[pl.ds(at, t_both.shape[1] // chunk)].reshape(t_both.shape[1], width)
-            for ref in (high, low))
+    def cross_of(t_both, x_high, x_low):
         product = dot(t_both, x_high)
         return product[:columns] + (product[columns:] + dot(t_both[:columns], x_low))
 
     def add_cross(at):
-        acc[...] += cross_of(turned[at], at)
+        acc[...] += cross_of(turned[at], high[at], low[at])
 
     def lay(out, first, sums):
         for side_at in range(width // 128):
@@ -337,11 +339,11 @@
         low[at] = x_low
         add_cross(at)
 
-    def first_half(c):
+    def first_half(c, rows=None):
         from_left(c).wait_recv()
-        pass_right(c).start()
+        pass_right(c, rows).start()
         from_right(half + c).wait_recv()
-        pass_left(c).start()
+        pass_left(c, rows).start()
         take(left * own + c)
         take(right * own + half + c)
 
@@ -351,11 +353,17 @@
             take(left * own + c)
             from_right(half + c).wait_recv()
             take(right * own + half + c)
-        for place, at in ((0, left * own + half - late), (1, right * own + own - late)):
+        for place, at in ((0, left * own + half), (1, right * own + own)):
             copy_y(guest.at[place], guest.at[place],
                    guest_send.at[place], guest_recv.at[place], right).wait_recv()
             t_both = jnp.concatenate(split(guest[place].T), axis=0)
-            lay(guest_out, place * columns, cross_of(t_both, at))
+            x_high, x_low = (
+                jnp.concatenate([
+                    ref[at - late - 1, chunk - cut :],
+                    ref[pl.ds(at - late, late)].reshape(late * chunk, width),
+                ], axis=0)
+                for ref in (high, low))
+            lay(guest_out, place * columns, cross_of(t_both, x_high, x_low))
         spread(slice_for(guest_out), guest_in, 5)
         guest_in[me] = mine(guest_out)
 
@@ -365,13 +373,24 @@
         from_right(c).wait_recv()
         take(right * own + c)
 
+    def keep_cut(at, rows):
+        x_high, x_low = split(held[at, rows])
+        high[at, rows] = x_high
+        low[at, rows] = x_low
+        return x_high, x_low
+
+    def take_cut(at):
+        x_high, x_low = keep_cut(at, slice(0, cut))
+        acc[...] += cross_of(turned[at, :, :cut], x_high, x_low)
+
     def passed(c):
         passed_left(c).wait_recv()
         take(across * own + c)
         passed_right(c).wait_recv()
         take(across * own + half + c)
 
-    loop(half - late, first_half)
+    loop(edge, first_half)
+    first_half(edge, 0)
     guests()
     loop(half, second_half)
     spread_wait(guest_in, 5)
@@ -380,7 +399,9 @@
     guest_sum[1] = sums[:, columns:]
     part_right().start()
     part_left().start()
-    for c in range(half - late, half):
+    pass_right(edge, 1).start()
+    pass_left(edge, 1).start()
+    for c in range(edge + 1, half):
         pass_right(c).start()
         pass_left(c).start()
 
@@ -391,7 +412,11 @@
     loop(own, finish)
     for copy in (guest_left(), guest_right()):
         copy.wait_send()
-    loop(half - late, passed)
+    loop(edge, passed)
+    passed_left(edge, 0).wait_recv()
+    take_cut(across * own + edge)
+    passed_right(edge, 0).wait_recv()
+    take_cut(across * own + half + edge)
 
     lay(cross_out, 0, acc[...])
     spread(slice_for(cross_out), cross_in, 3)
@@ -403,11 +428,12 @@
     cross_all[me] = jnp.sum(cross_in[...], axis=0) + (guest_part[0] + guest_part[1])
     spread(lambda to: cross_all.at[me], cross_all, 4)
 
-    def finish_passed(c):
-        pass_right(c).wait_send()
-        pass_left(c).wait_send()
-
-    loop(half - late, finish_passed)
+    def finish_passed(c, rows=None):
+        pass_right(c, rows).wait_send()
+        pass_left(c, rows).wait_send()
+
+    loop(edge, finish_passed)
+    finish_passed(edge, 0)
     for copy in (part_right(), part_left()):
         copy.wait_send()
     spread_wait(cross_all, 4)
@@ -415,31 +441,41 @@
     flat = cross_all[...].reshape(width, columns)
     cross = jnp.concatenate([flat[:columns], flat[columns:]], axis=1)
     x_high, x_low = split(cross)
-    product = dot_turned(both_high[...], jnp.concatenate([x_high, x_low], axis=0))
-    rest = product[:, columns:] + dot_turned(both_low[...], x_high)
-    solved = product[:, :columns] + rest
-    r_cross[...] = solved[:width]
-    coeff[...] = solved[width:]
-    weights = split_coeff(solved[width:])
+    x_both = jnp.concatenate([x_high, x_low], axis=0)
+
+    def solve(rows):
+        product = dot_turned(both_high[rows, :], x_both)
+        rest = product[:, columns:] + dot_turned(both_low[rows, :], x_high)
+        return product[:, :columns] + rest
+
+    solved = solve(slice(width, 2 * width))
+    coeff[...] = solved
+    weights = split_coeff(solved)
     each = chunks // STEPS
     for c in range(STEPS):
         if whole(c):
             trail[each * c : each * (c + 1)] = project(weights, trail, high, low, c)
+    r_cross[...] = solve(slice(0, width))
 
     def keep(at):
         high[at], low[at] = split(held[at])
 
-    for c in range(half - late, half):
+    passed_left(edge, 1).wait_recv()
+    keep_cut(across * own + edge, slice(cut, chunk))
+    passed_right(edge, 1).wait_recv()
+    keep_cut(across * own + half + edge, slice(cut, chunk))
+    for c in range(edge + 1, half):
         passed_left(c).wait_recv()
         keep(across * own + c)
         passed_right(c).wait_recv()
         keep(across * own + half + c)
 
-    loop(late, lambda c: finish_passed(half - late + c))
+    finish_passed(edge, 1)
+    loop(late, lambda c: finish_passed(edge + 1 + c))
 
 
 def residual_kernel(
-    r_factor_in, r_cross_in, coeff, trail, high, low, r_factor, r_cross, residual, staged, out_sem
+    r_factor_in, r_cross_in, coeff, trail, high, low, r_factor, r_cross, residual, staged, out_sem, small_sem
 ):
     each = trail.shape[0] // STEPS
 
@@ -451,18 +487,24 @@
     def rows_of(c):
         return trail.at[pl.ds(each * c, each)] if whole(c) else staged.at[c // 2]
 
+    small = (
+        pltpu.make_async_copy(r_factor_in, r_factor, small_sem.at[0]),
+        pltpu.make_async_copy(r_cross_in, r_cross, small_sem.at[1]),
+    )
     for c in range(STEPS):
         if whole(c):
             store(c, rows_of(c)).start()
+    for copy in small:
+        copy.start()
     weights = split_coeff(coeff[...])
     for c in range(STEPS):
         if not whole(c):
             staged[c // 2] = project(weights, trail, high, low, c)
             store(c, rows_of(c)).start()
-    r_factor[...] = r_factor_in[...]
-    r_cross[...] = r_cross_in[...]
     for c in range(STEPS):
         store(c, rows_of(c)).wait()
+    for copy in small:
+        copy.wait()
 
 
 def per_device(groups, chunk, late, panel, trailing):
@@ -503,18 +545,18 @@
             pltpu.VMEM((width, columns), f32),
             pltpu.VMEM((groups, part, columns), f32),
             pltpu.VMEM((groups, part, columns), f32),
-            pltpu.VMEM((2, late * chunk, columns), f32),
+            pltpu.VMEM((2, late * chunk + chunk // 2, columns), f32),
             pltpu.VMEM((width, 2 * columns), f32),
             pltpu.VMEM((groups, part, 2 * columns), f32),
             pltpu.VMEM((2, part, columns), f32),
             pltpu.VMEM((2, part, columns), f32),
             dma((own,)), dma((chunks,)),
             dma((own,)), dma((own,)), dma((own,)), dma((own,)),
-            dma((half,)), dma((half,)), dma((half,)), dma((half,)),
+            dma((half + 1,)), dma((half + 1,)), dma((half + 1,)), dma((half + 1,)),
             dma((6,)), dma((6,)), dma((2,)), dma((2,)), dma((2,)), dma((2,)), pltpu.SemaphoreType.REGULAR((5,)),
         ],
         compiler_params=pltpu.CompilerParams(
-            collective_id=0, has_side_effects=True, vmem_limit_bytes=30 * 2**20
+            collective_id=0, has_side_effects=True, vmem_limit_bytes=34 * 2**20
         ),
     )(panel, trailing)
     r_factor, r_cross, residual = pl.pallas_call(
@@ -525,8 +567,8 @@
             jax.ShapeDtypeStruct((chunks, chunk, columns), f32),
         ),
         in_specs=[vmem] * 6,
-        out_specs=(vmem, vmem, hbm),
-        scratch_shapes=[pltpu.VMEM((STEPS // 2, chunks // STEPS, chunk, columns), f32), dma((STEPS,))],
+        out_specs=(hbm,) * 3,
+        scratch_shapes=[pltpu.VMEM((STEPS // 2, chunks // STEPS, chunk, columns), f32), dma((STEPS,)), dma((2,))],
         compiler_params=pltpu.CompilerParams(vmem_limit_bytes=10 * 2**20),
     )(r_factor, r_cross, coeff, trail, high, low)
     return r_factor, r_cross, residual.reshape(total, columns)

time: 159 us -> 157 us (0.987)
  Pallas kernels: 158 us -> 156 us
where the time goes in v6:
time: 157 us
  Pallas kernels  156 us (99%)
    pallas_call x1, Pallas kernels, per_device(): pl.pallas_call(functools.partial(kernel, groups, ring, chunk, late), out_...  153 us
    pallas_call x1, Pallas kernels, per_device(): pl.pallas_call(residual_kernel, out_shape=(jax.ShapeDtypeStruct((width, w...  3.56 us

profile of v6, /device:TPU:1, one launch (start us, length us, event | category | flops | bytes accessed | tf_op | source)
XLA Modules:
  0.0 156.9 jit_solution(3717236378120642195)
XLA Ops:
  0.6 152.7 %shard_map.49 = (f32[256,256]{1,0:T(8,128)S(1)}, f32[256,128]{1,0:T(8,128)S(1)}, f32[256,128]{1,0:T(8,128)S(1)}, f32[32,512,128]{2,1,0:T(8,128)S(1)}, bf16[32,51...) custom-call(f32[4096,256]{1,0:T(8,128)} %panel.1, f32[16384,128]{1,0:T(8,128)} %trailing.1), custom_call_target="tpu_custom_call" | custom-call | tf_op jit(solution)/shard_map/pallas_call | solution.py:521
  153.3 3.6 %shard_map.50 = (f32[256,256]{1,0:T(8,128)}, f32[256,128]{1,0:T(8,128)}, f32[32,512,128]{2,1,0:T(8,128)}) custom-call(f32[256,256]{1,0:T(8,128)S(1)} %get-tuple-element.12.r_factor_in, f32[256,128]{1,0:T(8,128)S(1)} %get-tuple-element.13.r_cross_in, f32[256,128]{1,0:T(8,128)S(1)} %get-tuple-element.14.coeff, f32[32,512,128]{2,1,0:T(8,128)S(1)} %get-tuple-element.15.trail, ...), custom_call_target="tpu_custom_call" | custom-call | tf_op jit(solution)/shard_map/pallas_call | solution.py:562

commit v7 on v6

--- a/solution.py
+++ b/solution.py
@@ -227,7 +227,6 @@
     loop(chunks, lambda c: load_trail(c).start())
 
     gram[...] = jnp.zeros_like(gram)
-    both[...] = jnp.zeros_like(both)
 
     def gram_step(c):
         load_panel(c).wait()
@@ -236,15 +235,11 @@
         x_high, x_low = split(x)
         high[at] = x_high
         low[at] = x_low
-        x_turned = x.T.astype(jnp.bfloat16)
-        gram[...] += dot(x_turned, x_high)
-        both[:width, :] += dot(x_turned, x_low)
+        gram[...] += exact(x, x, ((0,), (0,)))
 
     loop(own, gram_step)
     pl.semaphore_wait(news.at[0], 2)
     tell_z(news.at[2])
-    mixed = both[:width, :]
-    gram[...] += mixed + mixed.T
 
     def spread(src_of, dst, stage):
         def one(to):

time: 157 us -> 157 us (level)
  no operation moved by 1% of the time
where the time goes in v7:
time: 157 us
  Pallas kernels  156 us (99%)
    pallas_call x1, Pallas kernels, per_device(): pl.pallas_call(functools.partial(kernel, groups, ring, chunk, late), out_...  153 us
    pallas_call x1, Pallas kernels, per_device(): pl.pallas_call(residual_kernel, out_shape=(jax.ShapeDtypeStruct((width, w...  3.56 us

profile of v7, /device:TPU:1, one launch (start us, length us, event | category | flops | bytes accessed | tf_op | source)
XLA Modules:
  0.0 156.9 jit_solution(288759095905211598)
XLA Ops:
  0.6 152.7 %shard_map.49 = (f32[256,256]{1,0:T(8,128)S(1)}, f32[256,128]{1,0:T(8,128)S(1)}, f32[256,128]{1,0:T(8,128)S(1)}, f32[32,512,128]{2,1,0:T(8,128)S(1)}, bf16[32,51...) custom-call(f32[4096,256]{1,0:T(8,128)} %panel.1, f32[16384,128]{1,0:T(8,128)} %trailing.1), custom_call_target="tpu_custom_call" | custom-call | tf_op jit(solution)/shard_map/pallas_call | solution.py:516
  153.3 3.6 %shard_map.50 = (f32[256,256]{1,0:T(8,128)}, f32[256,128]{1,0:T(8,128)}, f32[32,512,128]{2,1,0:T(8,128)}) custom-call(f32[256,256]{1,0:T(8,128)S(1)} %get-tuple-element.12.r_factor_in, f32[256,128]{1,0:T(8,128)S(1)} %get-tuple-element.13.r_cross_in, f32[256,128]{1,0:T(8,128)S(1)} %get-tuple-element.14.coeff, f32[32,512,128]{2,1,0:T(8,128)S(1)} %get-tuple-element.15.trail, ...), custom_call_target="tpu_custom_call" | custom-call | tf_op jit(solution)/shard_map/pallas_call | solution.py:557

commit v8 on v7

--- a/solution.py
+++ b/solution.py
@@ -11,6 +11,7 @@
 MESH = pl.DeviceIdType.MESH
 CHUNK = 512
 LATE = 1
+CUT = 2
 STEPS = 16
 BLOCK = 32
 
@@ -104,7 +105,7 @@
     early = max(own * 3 // 8, 1)
     chunks = trailing.shape[0] // chunk
     part = width // groups
-    edge, cut = half - late - 1, chunk // 2
+    edge, cut = half - late - 1, chunk // CUT
     late_rows = late * chunk + cut
     me = lax.axis_index("rows")
     y = lax.axis_index("cols")
@@ -132,6 +133,15 @@
         return at_xz(ring // 2 + i // (2 * ring), ring // 2 + lax.rem(i // 2, ring), lax.rem(i, 2))
 
     itself = (ring - ring // 2) * (2 * ring + 2)
+
+    far = sorted(
+        ((dx, dz, other) for dx in range(ring) for dz in range(ring) for other in range(2)),
+        key=lambda at: -min(at[0], ring - at[0]) - min(at[1], ring - at[1]))
+
+    def each_far(body):
+        for at in far:
+            if any(at):
+                body(at_xz(*at))
 
     def each_peer(body):
         loop(itself, lambda i: body(peer(i)))
@@ -187,7 +197,9 @@
                       send_l.at[c], recv_r.at[c], left)
 
     def piece(at, c, rows):
-        return held.at[at + c] if rows is None else held.at[at + c, pl.ds(rows * cut, cut)]
+        if rows is None:
+            return held.at[at + c]
+        return held.at[at + c, pl.ds(0, chunk - cut) if rows == 0 else pl.ds(chunk - cut, cut)]
 
     def pass_right(c, rows=None):
         ref, sem = piece(left * own, c, rows), half if rows == 1 else c
@@ -241,14 +253,14 @@
     pl.semaphore_wait(news.at[0], 2)
     tell_z(news.at[2])
 
-    def spread(src_of, dst, stage):
+    def spread(src_of, dst, stage, each=None):
         def one(to):
             pltpu.make_async_remote_copy(
                 src_ref=src_of(to), dst_ref=dst.at[me],
                 send_sem=small_send.at[stage], recv_sem=small_recv.at[stage],
                 device_id={"rows": to}, device_id_type=MESH).start()
 
-        each_peer(one)
+        (each or each_peer)(one)
 
     def spread_wait(dst, stage):
         some = dst.at[pl.ds(0, groups - 1)]
@@ -375,8 +387,8 @@
         return x_high, x_low
 
     def take_cut(at):
-        x_high, x_low = keep_cut(at, slice(0, cut))
-        acc[...] += cross_of(turned[at, :, :cut], x_high, x_low)
+        x_high, x_low = keep_cut(at, slice(0, chunk - cut))
+        acc[...] += cross_of(turned[at, :, : chunk - cut], x_high, x_low)
 
     def passed(c):
         passed_left(c).wait_recv()
@@ -394,11 +406,11 @@
     guest_sum[1] = sums[:, columns:]
     part_right().start()
     part_left().start()
-    pass_right(edge, 1).start()
-    pass_left(edge, 1).start()
     for c in range(edge + 1, half):
         pass_right(c).start()
         pass_left(c).start()
+    pass_right(edge, 1).start()
+    pass_left(edge, 1).start()
 
     def finish(c):
         to_right(c).wait_send()
@@ -414,14 +426,14 @@
     take_cut(across * own + half + edge)
 
     lay(cross_out, 0, acc[...])
-    spread(slice_for(cross_out), cross_in, 3)
+    spread(slice_for(cross_out), cross_in, 3, each_far)
     cross_in[me] = mine(cross_out)
     for place in range(2):
         copy_y(guest_part.at[place], guest_part.at[place],
                part_send.at[place], part_recv.at[place], right).wait_recv()
     spread_wait(cross_in, 3)
     cross_all[me] = jnp.sum(cross_in[...], axis=0) + (guest_part[0] + guest_part[1])
-    spread(lambda to: cross_all.at[me], cross_all, 4)
+    spread(lambda to: cross_all.at[me], cross_all, 4, each_far)
 
     def finish_passed(c, rows=None):
         pass_right(c, rows).wait_send()
@@ -455,15 +467,15 @@
     def keep(at):
         high[at], low[at] = split(held[at])
 
-    passed_left(edge, 1).wait_recv()
-    keep_cut(across * own + edge, slice(cut, chunk))
-    passed_right(edge, 1).wait_recv()
-    keep_cut(across * own + half + edge, slice(cut, chunk))
     for c in range(edge + 1, half):
         passed_left(c).wait_recv()
         keep(across * own + c)
         passed_right(c).wait_recv()
         keep(across * own + half + c)
+    passed_left(edge, 1).wait_recv()
+    keep_cut(across * own + edge, slice(chunk - cut, chunk))
+    passed_right(edge, 1).wait_recv()
+    keep_cut(across * own + half + edge, slice(chunk - cut, chunk))
 
     finish_passed(edge, 1)
     loop(late, lambda c: finish_passed(edge + 1 + c))
@@ -540,7 +552,7 @@
             pltpu.VMEM((width, columns), f32),
             pltpu.VMEM((groups, part, columns), f32),
             pltpu.VMEM((groups, part, columns), f32),
-            pltpu.VMEM((2, late * chunk + chunk // 2, columns), f32),
+            pltpu.VMEM((2, late * chunk + chunk // CUT, columns), f32),
             pltpu.VMEM((width, 2 * columns), f32),
             pltpu.VMEM((groups, part, 2 * columns), f32),
             pltpu.VMEM((2, part, columns), f32),

time: 157 us -> 157 us (level)
  no operation moved by 1% of the time
where the time goes in v8:
time: 157 us
  Pallas kernels  156 us (99%)
    pallas_call x1, Pallas kernels, per_device(): pl.pallas_call(functools.partial(kernel, groups, ring, chunk, late), out_...  153 us
    pallas_call x1, Pallas kernels, per_device(): pl.pallas_call(residual_kernel, out_shape=(jax.ShapeDtypeStruct((width, w...  3.56 us

profile of v8, /device:TPU:1, one launch (start us, length us, event | category | flops | bytes accessed | tf_op | source)
XLA Modules:
  0.0 156.8 jit_solution(4193804199164921290)
XLA Ops:
  0.6 152.6 %shard_map.49 = (f32[256,256]{1,0:T(8,128)S(1)}, f32[256,128]{1,0:T(8,128)S(1)}, f32[256,128]{1,0:T(8,128)S(1)}, f32[32,512,128]{2,1,0:T(8,128)S(1)}, bf16[32,51...) custom-call(f32[4096,256]{1,0:T(8,128)} %panel.1, f32[16384,128]{1,0:T(8,128)} %trailing.1), custom_call_target="tpu_custom_call" | custom-call | tf_op jit(solution)/shard_map/pallas_call | solution.py:528
  153.2 3.6 %shard_map.50 = (f32[256,256]{1,0:T(8,128)}, f32[256,128]{1,0:T(8,128)}, f32[32,512,128]{2,1,0:T(8,128)}) custom-call(f32[256,256]{1,0:T(8,128)S(1)} %get-tuple-element.12.r_factor_in, f32[256,128]{1,0:T(8,128)S(1)} %get-tuple-element.13.r_cross_in, f32[256,128]{1,0:T(8,128)S(1)} %get-tuple-element.14.coeff, f32[32,512,128]{2,1,0:T(8,128)S(1)} %get-tuple-element.15.trail, ...), custom_call_target="tpu_custom_call" | custom-call | tf_op jit(solution)/shard_map/pallas_call | solution.py:569
